TPU v7x, 32 devices: a whole 2x2x4 slice. The times are simulated.
32 devices in a mesh: dom: 4 (over z), dp: 8 (over y, x, core).
Axes of the slice: x: 2, y: 2, z: 4, core: 2. Of those that a mesh axis runs over, the one named last changes fastest.
Arguments:
- state: bfloat16 [8, 4096, 512], P('dp', 'dom'), may hold values from -6 to 6
- blocks: bfloat16 [32, 4, 128, 128], P('dom'), may hold values from -0.25 to 0.25
- source: int32 [32, 4], P('dom'), may hold values from 0 to 11
- count: int32 [32], P('dom'), may hold values from 1 to 4, as said below
- cotangent: bfloat16 [8, 4096, 512], P('dp', 'dom'), may hold values from -6 to 6
- w_self: bfloat16 [3, 512, 512], replicated, may hold values from -0.25 to 0.25
- w_nbr: bfloat16 [3, 512, 512], replicated, may hold values from -0.25 to 0.25
Outputs:
- final_state: bfloat16 [8, 4096, 512], P('dp', 'dom')
- state_grad: bfloat16 [8, 4096, 512], P('dp', 'dom')
- self_grad: float32 [3, 512, 512], replicated
- nbr_grad: float32 [3, 512, 512], replicated
Inputs may be any that keep to these rules, and one draw needn't show every extreme that they name: `source`: index into the partition's extended tiles: the last 2 tiles of the previous partition (cyclically), then its own 8 tiles, then the first 2 tiles of the next partition. Slots at or past the count are unused.
All inputs are finite; a program needn't handle non-finite values.
Results may differ from a plain program's by a relative error of at most 0.015.
Values may be sent and summed in bfloat16 or wider, within the bound.
A program may use at most 128 MiB of HBM per device.

v0:
```python
import math

import jax
import jax.numpy as jnp
from jax import lax
from jax.sharding import PartitionSpec as P

HALO = 2
LAYERS = 3


def with_halo(block, sides, width):
    for axis, dim in sides:
        count = lax.axis_size(axis)
        forward = [(i, i + 1) for i in range(count - 1)]
        forward.append((count - 1, 0))
        backward = [(target, source) for source, target in forward]
        low = lax.ppermute(
            lax.slice_in_dim(block, block.shape[dim] - width, None, axis=dim), axis, forward
        )
        high = lax.ppermute(lax.slice_in_dim(block, 0, width, axis=dim), axis, backward)
        block = jnp.concatenate([low, block, high], axis=dim)
    return block


def from_behind(block, axis, distance):
    devices = range(lax.axis_size(axis))
    route = [((i - distance) % len(devices), i) for i in devices]
    return lax.ppermute(block, axis, route)


def per_device(state, blocks, source, count, cotangent, w_self, w_nbr):
    tiles_dev, slots, tile_rows, _ = blocks.shape
    samples, node_rows, features = state.shape
    extent = tiles_dev + 2 * HALO
    rim_rows = HALO * tile_rows
    live_slots = (jnp.arange(slots, dtype=jnp.int32)[None, :] < count[:, None]).astype(jnp.bfloat16)
    weights_m = blocks * live_slots[:, :, None, None]
    chooser = (source[:, :, None] == jnp.arange(extent, dtype=jnp.int32)[None, None, :]).astype(
        jnp.float32
    )
    hidden = state
    inputs, aggregates, preacts = ([], [], [])
    for stratum in range(LAYERS):
        extended = with_halo(hidden, (("dom", 1),), rim_rows)
        ext_tiles = extended.reshape(samples, extent, tile_rows, features)
        gathered = jnp.take(ext_tiles, source, axis=1)
        aggregate = jnp.einsum(
            "tsab,ctsbf->ctaf", weights_m, gathered, preferred_element_type=jnp.float32
        )
        aggregate = aggregate.reshape(samples, node_rows, features).astype(jnp.bfloat16)
        preact = jnp.einsum(
            "crf,fg->crg", hidden, w_self[stratum], preferred_element_type=jnp.float32
        ) + jnp.einsum("crf,fg->crg", aggregate, w_nbr[stratum], preferred_element_type=jnp.float32)
        inputs.append(hidden)
        aggregates.append(aggregate)
        preacts.append(preact)
        hidden = (hidden.astype(jnp.float32) + jax.nn.silu(preact)).astype(jnp.bfloat16)
    grad_now = cotangent.astype(jnp.float32)
    self_parts, nbr_parts = ([], [])
    for stratum in reversed(range(LAYERS)):
        preact = preacts[stratum]
        sigmoid_pre = jax.nn.sigmoid(preact)
        grad_pre = (grad_now * sigmoid_pre * (1.0 + preact * (1.0 - sigmoid_pre))).astype(
            jnp.bfloat16
        )
        self_part = jnp.einsum(
            "crf,crg->fg", inputs[stratum], grad_pre, preferred_element_type=jnp.float32
        )
        nbr_part = jnp.einsum(
            "crf,crg->fg", aggregates[stratum], grad_pre, preferred_element_type=jnp.float32
        )
        self_parts.append(self_part)
        nbr_parts.append(nbr_part)
        grad_agg = jnp.einsum(
            "crg,fg->crf", grad_pre, w_nbr[stratum], preferred_element_type=jnp.float32
        ).astype(jnp.bfloat16)
        contrib = jnp.einsum(
            "tsba,ctaf->ctsbf",
            weights_m,
            grad_agg.reshape(samples, tiles_dev, tile_rows, features),
            preferred_element_type=jnp.float32,
        )
        ext_grad = jnp.einsum("tse,ctsbf->cebf", chooser, contrib, precision=lax.Precision.HIGHEST)
        ext_grad = ext_grad.reshape(samples, extent * tile_rows, features)
        left_rim = ext_grad[:, :rim_rows]
        right_rim = ext_grad[:, rim_rows + node_rows :]
        own_grad = ext_grad[:, rim_rows : rim_rows + node_rows]
        from_next = from_behind(left_rim.astype(jnp.bfloat16), "dom", -1).astype(left_rim.dtype)
        from_prev = from_behind(right_rim.astype(jnp.bfloat16), "dom", 1).astype(right_rim.dtype)
        own_grad = (
            own_grad
            + jnp.pad(from_prev, ((0, 0), (0, node_rows - rim_rows), (0, 0)))
            + jnp.pad(from_next, ((0, 0), (node_rows - rim_rows, 0), (0, 0)))
        )
        grad_now = (
            grad_now
            + jnp.einsum(
                "crg,fg->crf", grad_pre, w_self[stratum], preferred_element_type=jnp.float32
            )
            + own_grad
        )
    self_stack = jnp.stack(self_parts[::-1])
    nbr_stack = jnp.stack(nbr_parts[::-1])
    self_stack, nbr_stack = lax.psum((self_stack, nbr_stack), ("dom", "dp"))
    total_rows = samples * lax.axis_size("dp") * node_rows * lax.axis_size("dom")
    factor = 1.0 / math.sqrt(total_rows)
    return (hidden, grad_now.astype(jnp.bfloat16), self_stack * factor, nbr_stack * factor)


def solution(mesh):
    in_specs = (
        P("dp", "dom", None),
        P("dom", None, None, None),
        P("dom", None),
        P("dom"),
        P("dp", "dom", None),
        P(),
        P(),
    )
    out_specs = (P("dp", "dom", None), P("dp", "dom", None), P(), P())
    return jax.shard_map(
        per_device, mesh=mesh, in_specs=in_specs, out_specs=out_specs, check_vma=False
    )
```

profile of v0, /device:TPU:0, one launch (start us, length us, event | category | flops | bytes accessed | tf_op | source)
XLA Modules:
  0.0 359.6 jit_solution(3294379005037705617)
XLA Ops:
  8.3 3.1 collective-permute-start
  11.4 2.1 collective-permute-start.1
  15.0 3.4 fusion.55
  18.6 2.0 collective-permute-done
  20.6 4.2 %collective-permute-done.1 = bf16[1,256,512]{2,1,0:T(8,128)(2,1)S(1)} collective-permute-done((bf16[1,256,512]{2,1,0:T(8,128)(2,1)S(1)}, bf16[1,256,512]{2,1,0:T(8,128)(2,1)S(1)}, u32[]{:S(2)}, u32[]{:S(2)}) %collective-permute-start.1) | collective-permute-done | bytes 262176 | tf_op jit(solution)/shard_map/ppermute | solution.py:21
  24.9 2.8 gather_fusion
  27.7 3.5 bitcast_convert_fusion.2
  31.2 3.8 %fusion.25 = (bf16[1,1024,512]{2,1,0:T(8,128)(2,1)S(1)}, f32[1024,512]{1,0:T(8,128)}) fusion(bf16[1,1024,512]{2,1,0:T(8,128)(2,1)S(1)} %copy-done.2, f32[1024,512]{1,0:T(8,128)S(1)} %copy-done.11, bf16[1024,512]{1,0:T(8,128)(2,1)S(1)} %bitcast.283, bf16[3,512,512]{2,1,0:T(8,128)(2,1)} %param.15), kind=kOutput, calls=%fused_computation.52 | convolution fusion | flops 541065216 | bytes 7864320 | tf_op jit(solution)/shard_map/crf,fg->crg/dot_general | solution.py:54
  36.2 2.7 collective-permute-start.3
  38.9 3.1 fusion.52
  42.0 4.2 %collective-permute-done.2 = bf16[1,256,512]{2,1,0:T(8,128)(2,1)S(1)} collective-permute-done((bf16[1,256,512]{2,1,0:T(8,128)(2,1)S(1)}, bf16[1,256,512]{2,1,0:T(8,128)(2,1)S(1)}, u32[]{:S(2)}, u32[]{:S(2)}) %collective-permute-start.2) | collective-permute-done | bytes 262176 | tf_op jit(solution)/shard_map/ppermute | solution.py:18
  46.1 3.6 %collective-permute-done.3 = bf16[1,256,512]{2,1,0:T(8,128)(2,1)S(1)} collective-permute-done((bf16[1,256,512]{2,1,0:T(8,128)(2,1)S(1)}, bf16[1,256,512]{2,1,0:T(8,128)(2,1)S(1)}, u32[]{:S(2)}, u32[]{:S(2)}) %collective-permute-start.3) | collective-permute-done | bytes 262176 | tf_op jit(solution)/shard_map/ppermute | solution.py:21
  49.9 2.8 gather_fusion.1
  52.7 3.5 bitcast_convert_fusion.1
  56.2 3.8 %fusion.24 = (bf16[1,1024,512]{2,1,0:T(8,128)(2,1)S(1)}, f32[1024,512]{1,0:T(8,128)}) fusion(bf16[1,1024,512]{2,1,0:T(8,128)(2,1)S(1)} %copy-done.5, f32[1024,512]{1,0:T(8,128)S(1)} %copy-done.13, bf16[1024,512]{1,0:T(8,128)(2,1)S(1)} %bitcast.285, bf16[3,512,512]{2,1,0:T(8,128)(2,1)} %param.15), kind=kOutput, calls=%fused_computation.49 | convolution fusion | flops 541065216 | bytes 7864320 | tf_op jit(solution)/shard_map/crf,fg->crg/dot_general | solution.py:54
  60.5 3.6 %collective-permute-start.5 = (bf16[1,256,512]{2,1,0:T(8,128)(2,1)S(1)}, bf16[1,256,512]{2,1,0:T(8,128)(2,1)S(1)}, u32[]{:S(2)}, u32[]{:S(2)}) collective-permute-start(bf16[1,256,512]{2,1,0:T(8,128)(2,1)S(1)} %get-tuple-element.24), channel_id=1, source_target_pairs={{8,0},{16,8},{24,16},{0,24},{9,1},{17,9},{25,17},{1,25},{10,2},{18... | collective-permute-start | bytes 786440 | tf_op jit(solution)/shard_map/ppermute | solution.py:21
  64.1 3.1 fusion.49
  67.2 3.9 %collective-permute-done.4 = bf16[1,256,512]{2,1,0:T(8,128)(2,1)S(1)} collective-permute-done((bf16[1,256,512]{2,1,0:T(8,128)(2,1)S(1)}, bf16[1,256,512]{2,1,0:T(8,128)(2,1)S(1)}, u32[]{:S(2)}, u32[]{:S(2)}) %collective-permute-start.4) | collective-permute-done | bytes 262176 | tf_op jit(solution)/shard_map/ppermute | solution.py:18
  71.1 2.7 collective-permute-done.5
  73.9 2.8 gather_fusion.2
  76.7 3.5 bitcast_convert_fusion
  80.6 2.6 fusion.13
  84.2 4.7 %convolution_bitcast_fusion.2 = f32[8,4,128,512]{2,3,1,0:T(8,128)} fusion(bf16[8,128,512,1]{2,1,3,0:T(8,128)(2,1)S(1)} %bitcast.281, bf16[8,4,128,128]{3,2,1,0:T(8,128)(2,1)S(1)} %copy-done, bf16[8,4]{1,0:T(8,128)(2,1)S(1)} %fusion.92), kind=kOutput, calls=%fused_computation.17 | convolution fusion | flops 538968064 | bytes 10485824 | tf_op jit(solution)/shard_map/tsba,ctaf->ctsbf/dot_general | solution.py:78
  88.9 10.3 %copy.40 = f32[8,4,128,512]{3,0,1,2:T(8,128)} copy(f32[8,4,128,512]{2,3,1,0:T(8,128)} %convolution_bitcast_fusion.2) | data formatting | bytes 16777216 | tf_op jit(solution)/shard_map/reshape.41
  99.2 5.9 %convolution_bitcast_fusion.5 = f32[1,12,128,512]{3,1,2,0:T(8,128)S(1)} fusion(f32[8,4,128,512]{3,0,1,2:T(8,128)} %copy.40, s32[8,4]{0,1:T(4,128)S(1)} %copy-done.18), kind=kOutput, calls=%fused_computation.24 | convolution fusion | flops 301990272 | bytes 11534464 | tf_op jit(solution)/shard_map/tse,ctsbf->cebf/dot_general | solution.py:84
  107.9 3.4 collective-permute-start.7
  114.8 3.5 collective-permute-done.6
  118.3 2.4 collective-permute-done.7
  120.7 2.7 fusion.22
  126.2 4.7 %convolution_bitcast_fusion.1 = f32[8,4,128,512]{2,3,1,0:T(8,128)} fusion(bf16[8,128,512,1]{2,1,3,0:T(8,128)(2,1)S(1)} %bitcast.282, bf16[8,4,128,128]{3,2,1,0:T(8,128)(2,1)S(1)} %copy-done, bf16[8,4]{1,0:T(8,128)(2,1)S(1)} %fusion.92), kind=kOutput, calls=%fused_computation.16 | convolution fusion | flops 538968064 | bytes 10485824 | tf_op jit(solution)/shard_map/tsba,ctaf->ctsbf/dot_general | solution.py:78
  130.9 10.3 %copy.43 = f32[8,4,128,512]{3,0,1,2:T(8,128)} copy(f32[8,4,128,512]{2,3,1,0:T(8,128)} %convolution_bitcast_fusion.1) | data formatting | bytes 16777216 | tf_op jit(solution)/shard_map/reshape.49
  141.3 5.9 %convolution_bitcast_fusion.4 = f32[1,12,128,512]{3,1,2,0:T(8,128)S(1)} fusion(f32[8,4,128,512]{3,0,1,2:T(8,128)} %copy.43, s32[8,4]{0,1:T(4,128)S(1)} %copy-done.18), kind=kOutput, calls=%fused_computation.23 | convolution fusion | flops 301990272 | bytes 11534464 | tf_op jit(solution)/shard_map/tse,ctsbf->cebf/dot_general | solution.py:84
  150.4 2.9 collective-permute-start.9
  154.9 5.5 %collective-permute-done.8 = bf16[1,256,512]{2,1,0:T(8,128)(2,1)S(1)} collective-permute-done((bf16[1,256,512]{2,1,0:T(8,128)(2,1)S(1)}, bf16[1,256,512]{2,1,0:T(8,128)(2,1)S(1)}, u32[]{:S(2)}, u32[]{:S(2)}) %collective-permute-start.8) | collective-permute-done | bytes 262176 | tf_op jit(solution)/shard_map/ppermute | solution.py:29
  160.3 3.8 %collective-permute-done.9 = bf16[1,256,512]{2,1,0:T(8,128)(2,1)S(1)} collective-permute-done((bf16[1,256,512]{2,1,0:T(8,128)(2,1)S(1)}, bf16[1,256,512]{2,1,0:T(8,128)(2,1)S(1)}, u32[]{:S(2)}, u32[]{:S(2)}) %collective-permute-start.9) | collective-permute-done | bytes 262176 | tf_op jit(solution)/shard_map/ppermute | solution.py:29
  164.2 2.7 fusion.21
  169.8 2.0 pad_maximum_fusion.1
  173.8 2.1 convolution_convert_fusion
  175.9 5.1 %convolution_bitcast_fusion = f32[8,4,128,512]{2,3,1,0:T(8,128)} fusion(bf16[8,128,512,1]{2,1,3,0:T(8,128)(2,1)S(1)} %bitcast.280, bf16[8,4,128,128]{3,2,1,0:T(8,128)(2,1)S(1)} %copy-done, bf16[8,4]{1,0:T(8,128)(2,1)S(1)} %fusion.92), kind=kOutput, calls=%fused_computation.15 | convolution fusion | flops 538968064 | bytes 10485824 | tf_op jit(solution)/shard_map/tsba,ctaf->ctsbf/dot_general | solution.py:78
  180.9 10.4 %copy.46 = f32[8,4,128,512]{3,0,1,2:T(8,128)} copy(f32[8,4,128,512]{2,3,1,0:T(8,128)} %convolution_bitcast_fusion) | data formatting | bytes 16777216 | tf_op jit(solution)/shard_map/reshape.57
  191.3 5.9 %convolution_bitcast_fusion.3 = f32[1,12,128,512]{3,1,2,0:T(8,128)S(1)} fusion(f32[8,4,128,512]{3,0,1,2:T(8,128)} %copy.46, s32[8,4]{0,1:T(4,128)S(1)} %copy-done.18), kind=kOutput, calls=%fused_computation.22 | convolution fusion | flops 301990272 | bytes 11534464 | tf_op jit(solution)/shard_map/tse,ctsbf->cebf/dot_general | solution.py:84
  199.7 3.5 collective-permute-start.11
  203.2 12.8 %collective-permute-done.10 = bf16[1,256,512]{2,1,0:T(8,128)(2,1)S(1)} collective-permute-done((bf16[1,256,512]{2,1,0:T(8,128)(2,1)S(1)}, bf16[1,256,512]{2,1,0:T(8,128)(2,1)S(1)}, u32[]{:S(2)}, u32[]{:S(2)}) %collective-permute-start.10) | collective-permute-done | bytes 262176 | tf_op jit(solution)/shard_map/ppermute | solution.py:29
  216.0 3.8 %collective-permute-done.11 = bf16[1,256,512]{2,1,0:T(8,128)(2,1)S(1)} collective-permute-done((bf16[1,256,512]{2,1,0:T(8,128)(2,1)S(1)}, bf16[1,256,512]{2,1,0:T(8,128)(2,1)S(1)}, u32[]{:S(2)}, u32[]{:S(2)}) %collective-permute-start.11) | collective-permute-done | bytes 262176 | tf_op jit(solution)/shard_map/ppermute | solution.py:29
  221.5 119.2 %all-reduce.9.cloned.1.call-done = (f32[3,512,512]{1,2,0:T(8,128)}, f32[3,512,512]{1,2,0:T(8,128)}) async-done(((f32[3,512,512]{1,2,0:T(8,128)}, f32[3,512,512]{1,2,0:T(8,128)}), (f32[3,512,512]{1,2,0:T(8,128)}, f32[3,512,512]{1,2,0:T(8,128)})) %all-reduce.9.cloned.1.call-update) | async-done | bytes 6291472 | tf_op jit(solution)/shard_map/psum | solution.py:105
  340.7 5.7 %broadcast_multiply_fusion = (f32[3,512,512]{1,2,0:T(8,128)}, f32[3,512,512]{1,2,0:T(8,128)S(1)}) fusion(f32[3,512,512]{1,2,0:T(8,128)} %get-tuple-element.14, f32[3,512,512]{1,2,0:T(8,128)} %get-tuple-element.13), kind=kLoop, calls=%fused_computation.66 | loop fusion | flops 1572864 | bytes 12582912 | tf_op jit(solution)/shard_map/mul | solution.py:108
  346.4 3.5 copy.54
  349.9 2.4 copy.53
  (111 shorter events, 29.1 us)
Async XLA Ops:
  7.2 333.5 %all-reduce.9.cloned.1.call-start = ((), (), s32[]{:S(2)}) async-start(), calls=%async_computation | async-start | bytes 12582912 | tf_op jit(solution)/shard_map/psum | solution.py:105
  8.3 10.2 %copy-start.19 = (s32[8]{0:T(128)S(1)}, s32[8]{0:T(128)}, u32[]{:S(2)}) copy-start(s32[8]{0:T(128)} %param.12) | copy-start | bytes 100
  8.3 16.5 %copy-start.1 = (bf16[1,1024,512]{2,1,0:T(8,128)(2,1)S(1)}, bf16[1,1024,512]{2,1,0:T(8,128)(2,1)}, u32[]{:S(2)}) copy-start(bf16[1,1024,512]{2,1,0:T(8,128)(2,1)} %param.9) | copy-start | bytes 3145732
  8.3 12.3 %collective-permute-start = (bf16[1,256,512]{2,1,0:T(8,128)(2,1)S(1)}, bf16[1,256,512]{2,1,0:T(8,128)(2,1)S(1)}, u32[]{:S(2)}, u32[]{:S(2)}) collective-permute-start(bf16[1,256,512]{2,1,0:T(8,128)(2,1)S(1)} %get-tuple-element.27), channel_id=1, source_target_pairs={{0,8},{8,16},{16,24},{24,0},{1,9},{9,17},{17,25},{25,1},{2,10},{10... | collective-permute-start | bytes 786440 | tf_op jit(solution)/shard_map/ppermute | solution.py:18
  11.4 13.4 %collective-permute-start.1 = (bf16[1,256,512]{2,1,0:T(8,128)(2,1)S(1)}, bf16[1,256,512]{2,1,0:T(8,128)(2,1)S(1)}, u32[]{:S(2)}, u32[]{:S(2)}) collective-permute-start(bf16[1,256,512]{2,1,0:T(8,128)(2,1)S(1)} %get-tuple-element.28), channel_id=1, source_target_pairs={{8,0},{16,8},{24,16},{0,24},{9,1},{17,9},{25,17},{1,25},{10,2},{18... | collective-permute-start | bytes 786440 | tf_op jit(solution)/shard_map/ppermute | solution.py:21
  24.9 2.8 copy-start
  27.7 3.5 copy-start.2
  27.7 3.5 copy-start.11
  31.2 3.8 %copy-start.23 = (bf16[8,512,128]{1,2,0:T(8,128)(2,1)}, bf16[8,512,128]{1,2,0:T(8,128)(2,1)S(1)}, u32[]{:S(2)}) copy-start(bf16[8,512,128]{1,2,0:T(8,128)(2,1)S(1)} %bitcast_convert_fusion.2) | copy-start | bytes 3145732
  35.0 14.8 %copy-start.4 = (bf16[1,1024,512]{2,1,0:T(8,128)(2,1)}, bf16[1,1024,512]{2,1,0:T(8,128)(2,1)S(1)}, u32[]{:S(2)}) copy-start(bf16[1,1024,512]{2,1,0:T(8,128)(2,1)S(1)} %get-tuple-element.29) | copy-start | bytes 3145732
  35.1 11.1 %collective-permute-start.2 = (bf16[1,256,512]{2,1,0:T(8,128)(2,1)S(1)}, bf16[1,256,512]{2,1,0:T(8,128)(2,1)S(1)}, u32[]{:S(2)}, u32[]{:S(2)}) collective-permute-start(bf16[1,256,512]{2,1,0:T(8,128)(2,1)S(1)} %get-tuple-element.25), channel_id=1, source_target_pairs={{0,8},{8,16},{16,24},{24,0},{1,9},{9,17},{17,25},{25,1},{2,10},{10... | collective-permute-start | bytes 786440 | tf_op jit(solution)/shard_map/ppermute | solution.py:18
  36.2 13.6 %collective-permute-start.3 = (bf16[1,256,512]{2,1,0:T(8,128)(2,1)S(1)}, bf16[1,256,512]{2,1,0:T(8,128)(2,1)S(1)}, u32[]{:S(2)}, u32[]{:S(2)}) collective-permute-start(bf16[1,256,512]{2,1,0:T(8,128)(2,1)S(1)} %get-tuple-element.26), channel_id=1, source_target_pairs={{8,0},{16,8},{24,16},{0,24},{9,1},{17,9},{25,17},{1,25},{10,2},{18... | collective-permute-start | bytes 786440 | tf_op jit(solution)/shard_map/ppermute | solution.py:21
  52.7 3.5 copy-start.5
  52.7 3.5 copy-start.13
  56.2 3.8 %copy-start.25 = (bf16[8,512,128]{1,2,0:T(8,128)(2,1)}, bf16[8,512,128]{1,2,0:T(8,128)(2,1)S(1)}, u32[]{:S(2)}) copy-start(bf16[8,512,128]{1,2,0:T(8,128)(2,1)S(1)} %bitcast_convert_fusion.1) | copy-start | bytes 3145732
  60.0 13.8 %copy-start.7 = (bf16[1,1024,512]{2,1,0:T(8,128)(2,1)}, bf16[1,1024,512]{2,1,0:T(8,128)(2,1)S(1)}, u32[]{:S(2)}) copy-start(bf16[1,1024,512]{2,1,0:T(8,128)(2,1)S(1)} %get-tuple-element.31) | copy-start | bytes 3145732
  60.1 11.1 %collective-permute-start.4 = (bf16[1,256,512]{2,1,0:T(8,128)(2,1)S(1)}, bf16[1,256,512]{2,1,0:T(8,128)(2,1)S(1)}, u32[]{:S(2)}, u32[]{:S(2)}) collective-permute-start(bf16[1,256,512]{2,1,0:T(8,128)(2,1)S(1)} %get-tuple-element.23), channel_id=1, source_target_pairs={{0,8},{8,16},{16,24},{24,0},{1,9},{9,17},{17,25},{25,1},{2,10},{10... | collective-permute-start | bytes 786440 | tf_op jit(solution)/shard_map/ppermute | solution.py:18
  60.5 13.3 %collective-permute-start.5 = (bf16[1,256,512]{2,1,0:T(8,128)(2,1)S(1)}, bf16[1,256,512]{2,1,0:T(8,128)(2,1)S(1)}, u32[]{:S(2)}, u32[]{:S(2)}) collective-permute-start(bf16[1,256,512]{2,1,0:T(8,128)(2,1)S(1)} %get-tuple-element.24), channel_id=1, source_target_pairs={{8,0},{16,8},{24,16},{0,24},{9,1},{17,9},{25,17},{1,25},{10,2},{18... | collective-permute-start | bytes 786440 | tf_op jit(solution)/shard_map/ppermute | solution.py:21
  76.7 3.5 copy-start.8
  76.7 3.5 copy-start.12
  76.7 3.6 %copy-start.20 = (bf16[3,512,512]{2,1,0:T(8,128)(2,1)S(1)}, bf16[3,512,512]{2,1,0:T(8,128)(2,1)}, u32[]{:S(2)}) copy-start(bf16[3,512,512]{2,1,0:T(8,128)(2,1)} %param.15) | copy-start | bytes 4718596
  76.7 3.9 %copy-start.21 = (bf16[1,1024,512]{2,1,0:T(8,128)(2,1)S(1)}, bf16[1,1024,512]{2,1,0:T(8,128)(2,1)}, u32[]{:S(2)}) copy-start(bf16[1,1024,512]{2,1,0:T(8,128)(2,1)} %param.13) | copy-start | bytes 3145732
  80.2 3.0 copy-start.27
  83.2 1.0 copy-start.31
  88.9 10.3 %copy-start.18 = (s32[8,4]{0,1:T(4,128)S(1)}, s32[8,4]{0,1:T(4,128)}, u32[]{:S(2)}) copy-start(s32[8,4]{0,1:T(4,128)} %param.11) | copy-start | bytes 388
  106.9 4.3 %copy-start.32 = (bf16[1,1024,512]{2,1,0:T(8,128)(2,1)S(1)}, bf16[1,1024,512]{2,1,0:T(8,128)(2,1)}, u32[]{:S(2)}) copy-start(bf16[1,1024,512]{2,1,0:T(8,128)(2,1)} %copy-done.31) | copy-start | bytes 3145732
  107.2 11.1 %collective-permute-start.6 = (bf16[1,256,512]{2,1,0:T(8,128)(2,1)S(1)}, bf16[1,256,512]{2,1,0:T(8,128)(2,1)S(1)}, u32[]{:S(2)}, u32[]{:S(2)}) collective-permute-start(bf16[1,256,512]{2,1,0:T(8,128)(2,1)S(1)} %get-tuple-element.21), channel_id=1, source_target_pairs={{24,0},{0,8},{8,16},{16,24},{25,1},{1,9},{9,17},{17,25},{26,2},{2,... | collective-permute-start | bytes 786440 | tf_op jit(solution)/shard_map/ppermute | solution.py:29
  107.9 5.1 %copy-start.28 = (bf16[8,512,128]{1,2,0:T(8,128)(2,1)S(1)}, bf16[8,512,128]{1,2,0:T(8,128)(2,1)}, u32[]{:S(2)}) copy-start(bf16[8,512,128]{1,2,0:T(8,128)(2,1)} %copy-done.27) | copy-start | bytes 3145732
  107.9 12.8 %collective-permute-start.7 = (bf16[1,256,512]{2,1,0:T(8,128)(2,1)S(1)}, bf16[1,256,512]{2,1,0:T(8,128)(2,1)S(1)}, u32[]{:S(2)}, u32[]{:S(2)}) collective-permute-start(bf16[1,256,512]{2,1,0:T(8,128)(2,1)S(1)} %get-tuple-element.22), channel_id=1, source_target_pairs={{8,0},{16,8},{24,16},{0,24},{9,1},{17,9},{25,17},{1,25},{10,2},{18... | collective-permute-start | bytes 786440 | tf_op jit(solution)/shard_map/ppermute | solution.py:29
  113.0 7.7 %copy-start.9 = (bf16[3,512,512]{2,1,0:T(8,128)(2,1)S(1)}, bf16[3,512,512]{2,1,0:T(8,128)(2,1)}, u32[]{:S(2)}) copy-start(bf16[3,512,512]{2,1,0:T(8,128)(2,1)} %param.14) | copy-start | bytes 4718596
  113.0 7.7 %copy-start.22 = (bf16[1,1024,512]{2,1,0:T(8,128)(2,1)S(1)}, bf16[1,1024,512]{2,1,0:T(8,128)(2,1)}, u32[]{:S(2)}) copy-start(bf16[1,1024,512]{2,1,0:T(8,128)(2,1)} %param.13) | copy-start | bytes 3145732
  113.0 7.7 %copy-start.34 = (f32[1024,512]{1,0:T(8,128)S(1)}, f32[1024,512]{1,0:T(8,128)}, u32[]{:S(2)}) copy-start(f32[1024,512]{1,0:T(8,128)} %get-tuple-element.32) | copy-start | bytes 6291460
  123.4 1.0 copy-start.29
  149.0 4.4 %copy-start.6 = (bf16[1,1024,512]{2,1,0:T(8,128)(2,1)S(1)}, bf16[1,1024,512]{2,1,0:T(8,128)(2,1)}, u32[]{:S(2)}) copy-start(bf16[1,1024,512]{2,1,0:T(8,128)(2,1)} %copy-done.4) | copy-start | bytes 3145732
  149.0 4.3 %copy-start.30 = (bf16[1,1024,512]{2,1,0:T(8,128)(2,1)S(1)}, bf16[1,1024,512]{2,1,0:T(8,128)(2,1)}, u32[]{:S(2)}) copy-start(bf16[1,1024,512]{2,1,0:T(8,128)(2,1)} %copy-done.29) | copy-start | bytes 3145732
  149.2 11.1 %collective-permute-start.8 = (bf16[1,256,512]{2,1,0:T(8,128)(2,1)S(1)}, bf16[1,256,512]{2,1,0:T(8,128)(2,1)S(1)}, u32[]{:S(2)}, u32[]{:S(2)}) collective-permute-start(bf16[1,256,512]{2,1,0:T(8,128)(2,1)S(1)} %get-tuple-element.19), channel_id=1, source_target_pairs={{24,0},{0,8},{8,16},{16,24},{25,1},{1,9},{9,17},{17,25},{26,2},{2,... | collective-permute-start | bytes 786440 | tf_op jit(solution)/shard_map/ppermute | solution.py:29
  150.4 3.7 %copy-start.26 = (bf16[8,512,128]{1,2,0:T(8,128)(2,1)S(1)}, bf16[8,512,128]{1,2,0:T(8,128)(2,1)}, u32[]{:S(2)}) copy-start(bf16[8,512,128]{1,2,0:T(8,128)(2,1)} %copy-done.25) | copy-start | bytes 3145732
  150.4 13.8 %collective-permute-start.9 = (bf16[1,256,512]{2,1,0:T(8,128)(2,1)S(1)}, bf16[1,256,512]{2,1,0:T(8,128)(2,1)S(1)}, u32[]{:S(2)}, u32[]{:S(2)}) collective-permute-start(bf16[1,256,512]{2,1,0:T(8,128)(2,1)S(1)} %get-tuple-element.20), channel_id=1, source_target_pairs={{8,0},{16,8},{24,16},{0,24},{9,1},{17,9},{25,17},{1,25},{10,2},{18... | collective-permute-start | bytes 786440 | tf_op jit(solution)/shard_map/ppermute | solution.py:29
  154.1 10.1 %copy-start.33 = (f32[1024,512]{1,0:T(8,128)S(1)}, f32[1024,512]{1,0:T(8,128)}, u32[]{:S(2)}) copy-start(f32[1024,512]{1,0:T(8,128)} %get-tuple-element.30) | copy-start | bytes 6291460
  154.1 10.1 %copy-start.35 = (f32[1,1024,512]{2,1,0:T(8,128)S(1)}, f32[1,1024,512]{2,1,0:T(8,128)}, u32[]{:S(2)}) copy-start(f32[1,1024,512]{2,1,0:T(8,128)} %get-tuple-element.34) | copy-start | bytes 6291460
  164.2 2.7 copy-start.24
  166.9 1.6 copy-start.3
  168.5 1.2 copy-start.17
  169.8 2.0 copy-start.16
  199.1 20.7 %copy-start.10 = (f32[1,1024,512]{2,1,0:T(8,128)S(1)}, f32[1,1024,512]{2,1,0:T(8,128)}, u32[]{:S(2)}) copy-start(f32[1,1024,512]{2,1,0:T(8,128)} %get-tuple-element.36) | copy-start | bytes 6291460
  199.1 20.7 %copy-start.15 = (bf16[1,1024,512]{2,1,0:T(8,128)(2,1)S(1)}, bf16[1,1024,512]{2,1,0:T(8,128)(2,1)}, u32[]{:S(2)}) copy-start(bf16[1,1024,512]{2,1,0:T(8,128)(2,1)} %copy-done.14) | copy-start | bytes 3145732
  199.3 16.6 %collective-permute-start.10 = (bf16[1,256,512]{2,1,0:T(8,128)(2,1)S(1)}, bf16[1,256,512]{2,1,0:T(8,128)(2,1)S(1)}, u32[]{:S(2)}, u32[]{:S(2)}) collective-permute-start(bf16[1,256,512]{2,1,0:T(8,128)(2,1)S(1)} %get-tuple-element.17), channel_id=1, source_target_pairs={{24,0},{0,8},{8,16},{16,24},{25,1},{1,9},{9,17},{17,25},{26,2},{2,... | collective-permute-start | bytes 786440 | tf_op jit(solution)/shard_map/ppermute | solution.py:29
  199.7 20.0 %collective-permute-start.11 = (bf16[1,256,512]{2,1,0:T(8,128)(2,1)S(1)}, bf16[1,256,512]{2,1,0:T(8,128)(2,1)S(1)}, u32[]{:S(2)}, u32[]{:S(2)}) collective-permute-start(bf16[1,256,512]{2,1,0:T(8,128)(2,1)S(1)} %get-tuple-element.18), channel_id=1, source_target_pairs={{8,0},{16,8},{24,16},{0,24},{9,1},{17,9},{25,17},{1,25},{10,2},{18... | collective-permute-start | bytes 786440 | tf_op jit(solution)/shard_map/ppermute | solution.py:29
  (1 other events, 1.0 us)
Sparse Core Ops, SparseCore 0:
  173.9 166.7 all-reduce.8
where the time goes:
time: 366 us; the launch traced here: 360 us
  waiting for transfers between devices  172 us (47%)
  matrix products  80.6 us (22%)
  local copies, waits for them, and re-layouts  55.4 us (15%)
  starting transfers between devices  25.2 us (7%)
  between operations  14.9 us (4%)
  other arithmetic  11.9 us (3%)
    psum x1, waiting for transfers between devices, per_device(): self_stack, nbr_stack = lax.psum((self_stack, nbr_stack), ('dom', 'dp'))  119 us
    ppermute x6, waiting for transfers between devices, from_behind(): return lax.ppermute(block, axis, route)  31.8 us
    another operation x3, local copies, waits for them, and re-layouts  31 us
    dot_general x3, matrix products, per_device(): jnp.einsum('tse,ctsbf->cebf', chooser, contrib, precision=lax.Precision.H...  17.7 us
    dot_general x3, matrix products, per_device(): jnp.einsum('tsba,ctaf->ctsbf', weights_m, grad_agg.reshape(samples, tiles...  14.5 us
    ppermute x6, starting transfers between devices, from_behind(): return lax.ppermute(block, axis, route)  12 us
    ppermute x3, waiting for transfers between devices, with_halo(): lax.ppermute(lax.slice_in_dim(block, 0, width, axis=dim), axis, backward)  10.5 us
    dot_general x3, matrix products, per_device(): jnp.einsum('tsab,ctsbf->ctaf', weights_m, gathered, preferred_element_typ...  10.4 us
  transfers between devices with their start and end apart: 13, of which 13 were waited for; matrix products, arithmetic and copies ran while one was open for 12% of the time, Pallas kernels for 0%

commit v1 on v0

v1 whole, which is shorter than its diff:
```python
import functools
import math

import jax
import jax.numpy as jnp
from jax import lax
from jax.experimental import pallas as pl
from jax.experimental.pallas import tpu as pltpu
from jax.sharding import PartitionSpec as P

HALO = 2
LAYERS = 3
MESH = pl.DeviceIdType.MESH
F32 = jnp.float32
BF16 = jnp.bfloat16


def dot(a, b):
    return jnp.dot(a, b, preferred_element_type=F32)


def dot_nt(a, b):
    return lax.dot_general(a, b, (((1,), (1,)), ((), ())), preferred_element_type=F32)


def flip(x):
    return x.astype(F32).T.astype(BF16)


def kernel(
    n, k, state, blocks, source, count, cot, w_self, w_nbr,
    final, sgrad, gout,
    ext, adj, adj_back, hid_t, agg_t, agg_b, slope, pre_s, agg_s, grad, gpre, gagg,
    bsend, brecv, buf, rbuf, zbuf,
    fh_send, fh_recv, bh_send, bh_recv, rs_send, rs_recv, zr_send, zr_recv,
    zg_send, zg_recv, ag_send, ag_recv,
):
    dom, dp = lax.axis_index("dom"), lax.axis_index("dp")
    tiles, slots, tb, _ = blocks.shape
    rows, feat = state.shape
    rim = HALO * tb
    ext_tiles = tiles + 2 * HALO
    chunks = rows // rim
    wide = 2 * feat
    own = pl.ds(rim, rows)
    nxt = lax.rem(dom + 1, n)
    prv = lax.rem(dom + n - 1, n)

    def chunk(c):
        return pl.ds(pl.multiple_of(c * rim, rim), rim)

    def ext_chunk(c):
        return pl.ds(pl.multiple_of((c + 1) * rim, rim), rim)

    def bit_of(b):
        return lax.rem(lax.div(dp, 1 << b), 2)

    def partner(b):
        return dp + (1 - 2 * bit_of(b)) * (1 << b)

    barrier = pltpu.get_barrier_semaphore()
    for j in range(1, n):
        pl.semaphore_signal(
            barrier, inc=1, device_id={"dom": lax.rem(dom + j, n)}, device_id_type=MESH
        )
    for b in range(k):
        pl.semaphore_signal(barrier, inc=1, device_id={"dp": partner(b)}, device_id_type=MESH)
    pl.semaphore_wait(barrier, n - 1 + k)

    def remote(src, dst, send, recv, where):
        copy = pltpu.make_async_remote_copy(
            src_ref=src, dst_ref=dst, send_sem=send, recv_sem=recv,
            device_id=where, device_id_type=MESH,
        )
        copy.start()
        return copy

    def send_low(l, src):
        return remote(
            src, ext.at[l, pl.ds(rim + rows, rim)], fh_send.at[l, 0], fh_recv.at[l, 0],
            {"dom": prv},
        )

    def send_high(l, src):
        return remote(
            src, ext.at[l, pl.ds(0, rim)], fh_send.at[l, 1], fh_recv.at[l, 1], {"dom": nxt}
        )

    halo = [
        send_low(0, state.at[pl.ds(0, rim)]),
        send_high(0, state.at[pl.ds(rows - rim, rim)]),
    ]

    def load_state(c, _):
        ext[0, ext_chunk(c)] = state[chunk(c)]
        return 0

    lax.fori_loop(0, chunks, load_state, 0)

    def build(t, _):
        live = count[t]
        t_rows = pl.ds(pl.multiple_of(t * tb, tb), tb)
        weights = [blocks[t, s].astype(F32) for s in range(slots)]
        for u in range(ext_tiles):
            tile = jnp.zeros((tb, tb), F32)
            for s in range(slots):
                use = jnp.where((source[t, s] == u) & (live > s), 1.0, 0.0).astype(F32)
                tile = tile + weights[s] * use
            adj[t_rows, pl.ds(u * tb, tb)] = tile.astype(BF16)
            adj_back[pl.ds(u * tb, tb), t_rows] = tile.astype(BF16)
        return 0

    lax.fori_loop(0, tiles, build, 0)

    def finish(l, c):
        r, e = chunk(c), ext_chunk(c)
        agg = (
            agg_s[r]
            + dot(adj[r, pl.ds(0, rim)], ext[l, pl.ds(0, rim)])
            + dot(adj[r, pl.ds(rim + rows, rim)], ext[l, pl.ds(rim + rows, rim)])
        ).astype(BF16)
        agg_b[r] = agg
        pre = pre_s[r] + dot(agg, w_nbr[l])
        sig = jax.nn.sigmoid(pre)
        slope[l, r] = sig * (1.0 + pre * (1.0 - sig))
        hidden = (ext[l, e].astype(F32) + pre * sig).astype(BF16)
        if l < LAYERS - 1:
            ext[l + 1, e] = hidden
        else:
            final[r] = hidden

    def flip_agg(l):
        def body(c, _):
            agg_t[l, :, chunk(c)] = flip(agg_b[chunk(c)])
            return 0

        lax.fori_loop(0, chunks, body, 0)

    for l in range(LAYERS):
        if l > 0:
            flip_agg(l - 1)

        def before(c, _):
            r, e = chunk(c), ext_chunk(c)
            mine = ext[l, e]
            pre_s[r] = dot(mine, w_self[l])
            agg_s[r] = dot(adj[r, own], ext[l, own])
            hid_t[l, :, r] = flip(mine)
            return 0

        lax.fori_loop(0, chunks, before, 0)
        for copy in halo:
            copy.wait()
        halo = []
        finish(l, 0)
        if l < LAYERS - 1:
            halo.append(send_low(l + 1, ext.at[l + 1, pl.ds(rim, rim)]))
        finish(l, chunks - 1)
        if l < LAYERS - 1:
            halo.append(send_high(l + 1, ext.at[l + 1, pl.ds(rows, rim)]))

        def middle(c, _):
            finish(l, c)
            return 0

        lax.fori_loop(1, chunks - 1, middle, 0)

    half_cols = feat // 2
    rest = list(range(1, k))
    orders = ([0] + rest, [0] + rest[::-1])

    def summed(l):
        offs = [[0], [0]]
        lens = [wide >> s for s in range(k + 1)]
        for s in range(k + 1):
            flights = []
            if s < k:
                size = lens[s + 1]
                for q in range(2):
                    bit, off = bit_of(orders[q][s]), offs[q][s]
                    give = pl.multiple_of(off + (1 - bit) * size, size)
                    cols = pl.ds(q * half_cols, half_cols)
                    flights.append(
                        remote(
                            buf.at[l, pl.ds(give, size), cols],
                            rbuf.at[l, pl.ds(wide - lens[s], size), cols],
                            rs_send.at[l, q, s], rs_recv.at[l, q, s],
                            {"dp": partner(orders[q][s])},
                        )
                    )
                    offs[q].append(pl.multiple_of(off + bit * size, size))
                yield
                for copy in flights:
                    copy.wait()
                for q in range(2):
                    cols = pl.ds(q * half_cols, half_cols)
                    keep = pl.ds(offs[q][s + 1], size)
                    got = rbuf[l, pl.ds(wide - lens[s], size), cols].astype(F32)
                    buf[l, keep, cols] = (buf[l, keep, cols].astype(F32) + got).astype(BF16)
        piece_rows = zbuf.shape[3]
        across = half_cols // zbuf.shape[4]

        def piece(q, j):
            row = offs[q][k] + lax.div(j, across) * piece_rows
            col = q * half_cols + lax.rem(j, across) * zbuf.shape[4]
            return (
                pl.ds(pl.multiple_of(row, piece_rows), piece_rows),
                pl.ds(pl.multiple_of(col, zbuf.shape[4]), zbuf.shape[4]),
            )

        flights = []
        for j in range(1, n):
            peer = lax.rem(dom + j, n)
            for q in range(2):
                pr, pc = piece(q, peer)
                flights.append(
                    remote(
                        buf.at[l, pr, pc], zbuf.at[l, q, j],
                        zr_send.at[l, q, j], zr_recv.at[l, q, j], {"dom": peer},
                    )
                )
        yield
        for copy in flights:
            copy.wait()
        flights = []
        for q in range(2):
            pr, pc = piece(q, dom)
            total = buf[l, pr, pc].astype(F32)
            for j in range(1, n):
                total = total + zbuf[l, q, j].astype(F32)
            gout[l, pr, pc] = total.astype(BF16)
            for j in range(1, n):
                flights.append(
                    remote(
                        gout.at[l, pr, pc], gout.at[l, pr, pc],
                        zg_send.at[l, q, j], zg_recv.at[l, q, j],
                        {"dom": lax.rem(dom + j, n)},
                    )
                )
        yield
        for copy in flights:
            copy.wait()
        for s in reversed(range(k)):
            flights = []
            for q in range(2):
                where = (
                    l, pl.ds(offs[q][s + 1], lens[s + 1]), pl.ds(q * half_cols, half_cols)
                )
                flights.append(
                    remote(
                        gout.at[where], gout.at[where],
                        ag_send.at[l, q, s], ag_recv.at[l, q, s],
                        {"dp": partner(orders[q][s])},
                    )
                )
            yield
            for copy in flights:
                copy.wait()

    def advance(steps, times):
        for _ in range(times):
            next(steps, None)

    def load_cot(c, _):
        grad[chunk(c)] = cot[chunk(c)].astype(F32)
        return 0

    lax.fori_loop(0, chunks, load_cot, 0)

    def push(l, c):
        r = chunk(c)
        g = (grad[r] * slope[l, r]).astype(BF16)
        gpre[r] = g
        gagg[r] = dot_nt(g, w_nbr[l]).astype(BF16)

    def receive(l, flights):
        for copy in flights:
            copy.wait()
        first, last = pl.ds(0, rim), pl.ds(rows - rim, rim)
        grad[first] = grad[first] + brecv[l, 0].astype(F32)
        grad[last] = grad[last] + brecv[l, 1].astype(F32)

    halo, older = [], iter(())
    for l in reversed(range(LAYERS)):

        def inner(c, _):
            push(l, c)
            return 0

        lax.fori_loop(1, chunks - 1, inner, 0)
        if l < LAYERS - 1:
            receive(l + 1, halo)
        push(l, 0)
        push(l, chunks - 1)
        bsend[l, 0] = dot(adj_back[pl.ds(0, rim)], gagg[...]).astype(BF16)
        halo = [
            remote(
                bsend.at[l, 0], brecv.at[l, 1], bh_send.at[l, 0], bh_recv.at[l, 0],
                {"dom": prv},
            )
        ]
        bsend[l, 1] = dot(adj_back[pl.ds(rim + rows, rim)], gagg[...]).astype(BF16)
        halo.append(
            remote(
                bsend.at[l, 1], brecv.at[l, 0], bh_send.at[l, 1], bh_recv.at[l, 1],
                {"dom": nxt},
            )
        )
        advance(older, 1)
        if l == LAYERS - 1:
            flip_agg(l)

        def weights(c, _):
            r = chunk(c)
            buf[l, r] = dot(hid_t[l, r], gpre[...]).astype(BF16)
            buf[l, pl.ds(pl.multiple_of(feat + c * rim, rim), rim)] = dot(
                agg_t[l, r], gpre[...]
            ).astype(BF16)
            return 0

        lax.fori_loop(0, feat // rim, weights, 0)
        newer = summed(l)
        advance(newer, 1)
        advance(older, 1)

        def onward(c, _):
            r = chunk(c)
            grad[r] = grad[r] + dot_nt(gpre[r], w_self[l]) + dot(adj_back[ext_chunk(c)], gagg[...])
            return 0

        lax.fori_loop(0, chunks, onward, 0)
        for _ in range(k):
            advance(newer, 1)
            advance(older, 1)
        for _ in older:
            pass
        older = newer
    receive(0, halo)

    def store(c, _):
        sgrad[chunk(c)] = grad[chunk(c)].astype(BF16)
        return 0

    lax.fori_loop(0, chunks, store, 0)
    for _ in older:
        pass


def per_device(n, d, state, blocks, source, count, cotangent, w_self, w_nbr):
    tiles, slots, tb, _ = blocks.shape
    samples, rows, feat = state.shape
    rim = HALO * tb
    extent = rows + 2 * rim
    wide = 2 * feat
    k = d.bit_length() - 1
    across = feat // 2 // 128
    piece_rows = (wide >> k) // (n // across)
    vmem = pl.BlockSpec(memory_space=pltpu.VMEM)
    smem = pl.BlockSpec(memory_space=pltpu.SMEM)
    dma = pltpu.SemaphoreType.DMA
    scratch = [
        pltpu.VMEM((LAYERS, extent, feat), BF16),
        pltpu.VMEM((rows, extent), BF16),
        pltpu.VMEM((extent, rows), BF16),
        pltpu.VMEM((LAYERS, feat, rows), BF16),
        pltpu.VMEM((LAYERS, feat, rows), BF16),
        pltpu.VMEM((rows, feat), BF16),
        pltpu.VMEM((LAYERS, rows, feat), F32),
        pltpu.VMEM((rows, feat), F32),
        pltpu.VMEM((rows, feat), F32),
        pltpu.VMEM((rows, feat), F32),
        pltpu.VMEM((rows, feat), BF16),
        pltpu.VMEM((rows, feat), BF16),
        pltpu.VMEM((LAYERS, 2, rim, feat), BF16),
        pltpu.VMEM((LAYERS, 2, rim, feat), BF16),
        pltpu.VMEM((LAYERS, wide, feat), BF16),
        pltpu.VMEM((LAYERS, wide, feat), BF16),
        pltpu.VMEM((LAYERS, 2, n, piece_rows, 128), BF16),
        dma((LAYERS, 2)), dma((LAYERS, 2)), dma((LAYERS, 2)), dma((LAYERS, 2)),
        dma((LAYERS, 2, k)), dma((LAYERS, 2, k)),
        dma((LAYERS, 2, n)), dma((LAYERS, 2, n)),
        dma((LAYERS, 2, n)), dma((LAYERS, 2, n)),
        dma((LAYERS, 2, k)), dma((LAYERS, 2, k)),
    ]
    final, sgrad, gout = pl.pallas_call(
        functools.partial(kernel, n, k),
        out_shape=(
            jax.ShapeDtypeStruct((rows, feat), BF16),
            jax.ShapeDtypeStruct((rows, feat), BF16),
            jax.ShapeDtypeStruct((LAYERS, wide, feat), BF16),
        ),
        in_specs=[vmem, vmem, smem, smem, vmem, vmem, vmem],
        out_specs=(vmem, vmem, vmem),
        scratch_shapes=scratch,
        compiler_params=pltpu.CompilerParams(
            collective_id=0, has_side_effects=True, vmem_limit_bytes=60 * 1024 * 1024
        ),
    )(
        state.reshape(samples * rows, feat), blocks, source, count,
        cotangent.reshape(samples * rows, feat), w_self, w_nbr,
    )
    factor = 1.0 / math.sqrt(rows * samples * n * d)
    grads = gout.astype(F32) * factor
    return final[None], sgrad[None], grads[:, :feat], grads[:, feat:]


def solution(mesh):
    in_specs = (
        P("dp", "dom", None),
        P("dom", None, None, None),
        P("dom", None),
        P("dom"),
        P("dp", "dom", None),
        P(),
        P(),
    )
    out_specs = (P("dp", "dom", None), P("dp", "dom", None), P(), P())
    return jax.shard_map(
        functools.partial(per_device, mesh.shape["dom"], mesh.shape["dp"]),
        mesh=mesh, in_specs=in_specs, out_specs=out_specs, check_vma=False,
    )
```

time: 366 us -> 155 us (0.42); the launches traced: 360 us -> 155 us
  waiting for transfers between devices: 172 us -> 0 us
  Pallas kernels: 0 us -> 144 us
  matrix products: 80.6 us -> 0 us
  local copies, waits for them, and re-layouts: 55.4 us -> 6.73 us
  starting transfers between devices: 25.2 us -> 0 us
  between operations: 14.9 us -> 0.66 us
  other arithmetic: 11.9 us -> 2.82 us
    pallas_call x0 -> x1, Pallas kernels: none -> 144 us  [per_device(): pl.pallas_call(functools.partial(kernel, n, k), out_shape=(jax.ShapeDtype...]
    psum x1 -> x0, waiting for transfers between devices: 119 us -> none  [per_device(): self_stack, nbr_stack = lax.psum((self_stack, nbr_stack), ('dom', 'dp'))]
    dot_general x27 -> x0, matrix products: 80.6 us -> none  [the longest x3 17.7 us: per_device(): jnp.einsum('tse,ctsbf->cebf', chooser, contrib, precision=lax.Precision.H...]
    ppermute x12 -> x0, waiting for transfers between devices: 52.4 us -> none  [the longest x6 31.8 us: from_behind(): return lax.ppermute(block, axis, route)]
    another operation x3 -> x0, local copies, waits for them, and re-layouts: 31 us -> none
    ppermute x12 -> x0, starting transfers between devices: 25.1 us -> none  [the longest x6 12 us: from_behind(): return lax.ppermute(block, axis, route)]
    gather x3 -> x0, local copies, waits for them, and re-layouts: 8.46 us -> none  [per_device(): gathered = jnp.take(ext_tiles, source, axis=1)]
    unnamed x74 -> x7, local copies, waits for them, and re-layouts: 8.99 us -> 3.3 us
  transfers between devices with their start and end apart: 13 -> 0, of which waited for: 13 -> 0; matrix products, arithmetic and copies ran while one was open for 12% -> 0% of each run, Pallas kernels for 0% -> 0%
where the time goes in v1:
time: 155 us
  Pallas kernels  144 us (93%)
  local copies, waits for them, and re-layouts  6.73 us (4%)
  other arithmetic  2.82 us (2%)
    pallas_call x1, Pallas kernels, per_device(): pl.pallas_call(functools.partial(kernel, n, k), out_shape=(jax.ShapeDtype...  144 us
    slice x1, local copies, waits for them, and re-layouts, per_device(): return (final[None], sgrad[None], grads[:, :feat], grads[:, feat:])  3.43 us
    unnamed x7, local copies, waits for them, and re-layouts  3.3 us

profile of v1, /device:TPU:0, one launch (start us, length us, event | category | flops | bytes accessed | tf_op | source)
XLA Modules:
  0.0 154.5 jit_solution(13139731024950741634)
XLA Ops:
  0.6 1.3 copy.11.source
  2.0 144.3 %shard_map.102 = (bf16[1024,512]{1,0:T(8,128)(2,1)}, bf16[1024,512]{1,0:T(8,128)(2,1)}, bf16[3,1024,512]{2,1,0:T(8,128)(2,1)}) custom-call(bf16[1024,512]{1,0:T(8,128)(2,1)} %bitcast.6, bf16[8,4,128,128]{3,2,1,0:T(8,128)(2,1)} %blocks.1, s32[8,4]{1,0:T(8,128)} %copy.11.source, s32[8]{0:T(128)} %count.1, bf16[1024,512]{1,0:T(8,128)(2,1)} %bitcast.7, ...), custom_call_target="tpu_custom_call" | custom-call | tf_op jit(solution)/shard_map/pallas_call | solution.py:385
  146.3 2.8 %convert_multiply_fusion = f32[3,1024,512]{2,1,0:T(8,128)S(1)} fusion(bf16[3,1024,512]{2,1,0:T(8,128)(2,1)} %get-tuple-element.9), kind=kLoop, calls=%fused_computation | loop fusion | flops 3145728 | bytes 9437184 | tf_op jit(solution)/shard_map/mul | solution.py:403
  149.1 0.0 copy-start.1
  149.2 0.0 copy-start
  149.2 3.4 %fusion = (f32[3,512,512]{2,1,0:T(8,128)}, f32[3,512,512]{2,1,0:T(8,128)}) fusion(f32[3,1024,512]{2,1,0:T(8,128)S(1)} %convert_multiply_fusion), kind=kLoop, calls=%fused_computation.1 | loop fusion | bytes 12582912 | tf_op jit(solution)/shard_map/slice | solution.py:404
  152.6 0.0 copy-done.1
  152.6 1.0 copy.14
  153.6 0.0 copy-done
  153.6 1.0 copy.15
Async XLA Ops:
  149.1 3.5 %copy-start.1 = (bf16[1024,512]{1,0:T(8,128)(2,1)S(1)}, bf16[1024,512]{1,0:T(8,128)(2,1)}, u32[]{:S(2)}) copy-start(bf16[1024,512]{1,0:T(8,128)(2,1)} %get-tuple-element.7) | copy-start | bytes 3145732
  149.2 4.4 %copy-start = (bf16[1024,512]{1,0:T(8,128)(2,1)S(1)}, bf16[1024,512]{1,0:T(8,128)(2,1)}, u32[]{:S(2)}) copy-start(bf16[1024,512]{1,0:T(8,128)(2,1)} %get-tuple-element.8) | copy-start | bytes 3145732

commit v2 on v1

--- a/solution.py
+++ b/solution.py
@@ -280,7 +280,21 @@
         grad[first] = grad[first] + brecv[l, 0].astype(F32)
         grad[last] = grad[last] + brecv[l, 1].astype(F32)
 
-    halo, older = [], iter(())
+    def weigh(l):
+        def weights(c, _):
+            r = chunk(c)
+            buf[l, r] = dot(hid_t[l, r], gpre[...]).astype(BF16)
+            buf[l, pl.ds(pl.multiple_of(feat + c * rim, rim), rim)] = dot(
+                agg_t[l, r], gpre[...]
+            ).astype(BF16)
+            return 0
+
+        lax.fori_loop(0, feat // rim, weights, 0)
+        steps = summed(l)
+        advance(steps, 1)
+        return steps
+
+    halo, older, oldest = [], iter(()), iter(())
     for l in reversed(range(LAYERS)):
 
         def inner(c, _):
@@ -292,6 +306,8 @@
             receive(l + 1, halo)
         push(l, 0)
         push(l, chunks - 1)
+        if l == 0:
+            newer = weigh(l)
         bsend[l, 0] = dot(adj_back[pl.ds(0, rim)], gagg[...]).astype(BF16)
         halo = [
             remote(
@@ -307,21 +323,14 @@
             )
         )
         advance(older, 1)
+        advance(oldest, 1)
         if l == LAYERS - 1:
             flip_agg(l)
-
-        def weights(c, _):
-            r = chunk(c)
-            buf[l, r] = dot(hid_t[l, r], gpre[...]).astype(BF16)
-            buf[l, pl.ds(pl.multiple_of(feat + c * rim, rim), rim)] = dot(
-                agg_t[l, r], gpre[...]
-            ).astype(BF16)
-            return 0
-
-        lax.fori_loop(0, feat // rim, weights, 0)
-        newer = summed(l)
-        advance(newer, 1)
-        advance(older, 1)
+        if l == 0:
+            advance(newer, 1)
+        else:
+            newer = weigh(l)
+        advance(oldest, 1)
 
         def onward(c, _):
             r = chunk(c)
@@ -329,12 +338,15 @@
             return 0
 
         lax.fori_loop(0, chunks, onward, 0)
-        for _ in range(k):
+        for _ in range(k if l > 0 else k - 1):
             advance(newer, 1)
-            advance(older, 1)
-        for _ in older:
+            advance(oldest, 1)
+        for _ in oldest:
             pass
-        older = newer
+        if l > 0:
+            oldest, older = older, newer
+    advance(older, 1)
+    advance(newer, 1)
     receive(0, halo)
 
     def store(c, _):
@@ -342,8 +354,9 @@
         return 0
 
     lax.fori_loop(0, chunks, store, 0)
-    for _ in older:
-        pass
+    for _ in range(k + 1):
+        advance(older, 1)
+        advance(newer, 1)
 
 
 def per_device(n, d, state, blocks, source, count, cotangent, w_self, w_nbr):
@@ -400,8 +413,12 @@
         cotangent.reshape(samples * rows, feat), w_self, w_nbr,
     )
     factor = 1.0 / math.sqrt(rows * samples * n * d)
-    grads = gout.astype(F32) * factor
-    return final[None], sgrad[None], grads[:, :feat], grads[:, feat:]
+    return (
+        final[None],
+        sgrad[None],
+        gout[:, :feat].astype(F32) * factor,
+        gout[:, feat:].astype(F32) * factor,
+    )
 
 
 def solution(mesh):

time: 155 us -> 134 us (0.86)
  Pallas kernels: 144 us -> 124 us
  local copies, waits for them, and re-layouts: 6.73 us -> 3.3 us
  other arithmetic: 2.82 us -> 5.68 us
    pallas_call x1, Pallas kernels: 144 us -> 124 us  [per_device(): pl.pallas_call(functools.partial(kernel, n, k), out_shape=(jax.ShapeDtype...]
    slice x1 -> x0, local copies, waits for them, and re-layouts: 3.43 us -> none  [per_device(): return (final[None], sgrad[None], grads[:, :feat], grads[:, feat:])]
    mul x1, other arithmetic: 2.82 us -> 5.68 us  [per_device(): gout[:, feat:].astype(F32) * factor]
where the time goes in v2:
time: 134 us
  Pallas kernels  124 us (93%)
  other arithmetic  5.68 us (4%)
  local copies, waits for them, and re-layouts  3.3 us (2%)
    pallas_call x1, Pallas kernels, per_device(): pl.pallas_call(functools.partial(kernel, n, k), out_shape=(jax.ShapeDtype...  124 us
    mul x1, other arithmetic, per_device(): gout[:, feat:].astype(F32) * factor  5.68 us
    unnamed x7, local copies, waits for them, and re-layouts  3.3 us

profile of v2, /device:TPU:0, one launch (start us, length us, event | category | flops | bytes accessed | tf_op | source)
XLA Modules:
  0.0 133.8 jit_solution(3199342304377235762)
XLA Ops:
  0.6 1.3 %copy.11.source = s32[8,4]{1,0:T(8,128)} copy(s32[8,4]{0,1:T(4,128)} %param.9) | data formatting | bytes 256 | tf_op args[2]
  2.0 124.1 %shard_map.102 = (bf16[1024,512]{1,0:T(8,128)(2,1)}, bf16[1024,512]{1,0:T(8,128)(2,1)}, bf16[3,1024,512]{2,1,0:T(8,128)(2,1)}) custom-call(bf16[1024,512]{1,0:T(8,128)(2,1)} %bitcast.6, bf16[8,4,128,128]{3,2,1,0:T(8,128)(2,1)} %blocks.1, s32[8,4]{1,0:T(8,128)} %copy.11.source, s32[8]{0:T(128)} %count.1, bf16[1024,512]{1,0:T(8,128)(2,1)} %bitcast.7, ...), custom_call_target="tpu_custom_call" | custom-call | tf_op jit(solution)/shard_map/pallas_call | solution.py:398
  126.1 0.0 copy-start.1
  126.1 0.0 copy-start
  126.1 5.7 %convert_multiply_fusion = (f32[3,512,512]{2,1,0:T(8,128)}, f32[3,512,512]{2,1,0:T(8,128)}) fusion(bf16[3,1024,512]{2,1,0:T(8,128)(2,1)} %get-tuple-element.9), kind=kLoop, calls=%fused_computation | loop fusion | flops 3145728 | bytes 9437184 | tf_op jit(solution)/shard_map/mul | solution.py:420
  131.8 0.0 copy-done.1
  131.8 1.0 copy.14
  132.8 0.0 copy-done
  132.8 1.0 copy.15
Async XLA Ops:
  126.1 5.7 %copy-start.1 = (bf16[1024,512]{1,0:T(8,128)(2,1)S(1)}, bf16[1024,512]{1,0:T(8,128)(2,1)}, u32[]{:S(2)}) copy-start(bf16[1024,512]{1,0:T(8,128)(2,1)} %get-tuple-element.7) | copy-start | bytes 3145732
  126.1 6.7 %copy-start = (bf16[1024,512]{1,0:T(8,128)(2,1)S(1)}, bf16[1024,512]{1,0:T(8,128)(2,1)}, u32[]{:S(2)}) copy-start(bf16[1024,512]{1,0:T(8,128)(2,1)} %get-tuple-element.8) | copy-start | bytes 3145732

commit v3 on v2

--- a/solution.py
+++ b/solution.py
@@ -28,10 +28,10 @@
 
 
 def kernel(
-    n, k, state, blocks, source, count, cot, w_self, w_nbr,
+    n, k, state, blocks, source, count, cot_in, w_self_in, w_nbr_in,
     final, sgrad, gout,
     ext, adj, adj_back, hid_t, agg_t, agg_b, slope, pre_s, agg_s, grad, gpre, gagg,
-    bsend, brecv, buf, rbuf, zbuf,
+    bsend, brecv, buf, rbuf, zbuf, cot, w_self, w_nbr, load_sem,
     fh_send, fh_recv, bh_send, bh_recv, rs_send, rs_recv, zr_send, zr_recv,
     zg_send, zg_recv, ag_send, ag_recv,
 ):
@@ -58,6 +58,14 @@
     def partner(b):
         return dp + (1 - 2 * bit_of(b)) * (1 << b)
 
+    loads = [
+        pltpu.make_async_copy(w_self_in, w_self, load_sem.at[0]),
+        pltpu.make_async_copy(w_nbr_in, w_nbr, load_sem.at[1]),
+        pltpu.make_async_copy(cot_in, cot, load_sem.at[2]),
+    ]
+    for load in loads:
+        load.start()
+
     barrier = pltpu.get_barrier_semaphore()
     for j in range(1, n):
         pl.semaphore_signal(
@@ -111,6 +119,8 @@
         return 0
 
     lax.fori_loop(0, tiles, build, 0)
+    for load in loads:
+        load.wait()
 
     def finish(l, c):
         r, e = chunk(c), ext_chunk(c)
@@ -280,13 +290,31 @@
         grad[first] = grad[first] + brecv[l, 0].astype(F32)
         grad[last] = grad[last] + brecv[l, 1].astype(F32)
 
+    mid = pl.ds(rim, rows - 2 * rim)
+    ends = (pl.ds(0, rim), pl.ds(rows - rim, rim))
+    rims = (pl.ds(0, rim), pl.ds(rim + rows, rim))
+
+    def weigh_mid(l):
+        def weights(c, _):
+            r = chunk(c)
+            pre_s[r] = dot(hid_t[l, r, mid], gpre[mid])
+            pre_s[pl.ds(pl.multiple_of(feat + c * rim, rim), rim)] = dot(
+                agg_t[l, r, mid], gpre[mid]
+            )
+            return 0
+
+        lax.fori_loop(0, feat // rim, weights, 0)
+
     def weigh(l):
         def weights(c, _):
             r = chunk(c)
-            buf[l, r] = dot(hid_t[l, r], gpre[...]).astype(BF16)
-            buf[l, pl.ds(pl.multiple_of(feat + c * rim, rim), rim)] = dot(
-                agg_t[l, r], gpre[...]
-            ).astype(BF16)
+            low = pl.ds(pl.multiple_of(feat + c * rim, rim), rim)
+            top, bottom = pre_s[r], pre_s[low]
+            for end in ends:
+                top = top + dot(hid_t[l, r, end], gpre[end])
+                bottom = bottom + dot(agg_t[l, r, end], gpre[end])
+            buf[l, r] = top.astype(BF16)
+            buf[l, low] = bottom.astype(BF16)
             return 0
 
         lax.fori_loop(0, feat // rim, weights, 0)
@@ -294,6 +322,16 @@
         advance(steps, 1)
         return steps
 
+    def back_mid():
+        for i in range(2):
+            agg_s[pl.ds(i * rim, rim)] = dot(adj_back[rims[i], mid], gagg[mid])
+
+    def back(i):
+        total = agg_s[pl.ds(i * rim, rim)]
+        for end in ends:
+            total = total + dot(adj_back[rims[i], end], gagg[end])
+        return total.astype(BF16)
+
     halo, older, oldest = [], iter(()), iter(())
     for l in reversed(range(LAYERS)):
 
@@ -302,33 +340,36 @@
             return 0
 
         lax.fori_loop(1, chunks - 1, inner, 0)
+        back_mid()
         if l < LAYERS - 1:
+            weigh_mid(l)
             receive(l + 1, halo)
         push(l, 0)
         push(l, chunks - 1)
         if l == 0:
             newer = weigh(l)
-        bsend[l, 0] = dot(adj_back[pl.ds(0, rim)], gagg[...]).astype(BF16)
+        bsend[l, 0] = back(0)
         halo = [
             remote(
                 bsend.at[l, 0], brecv.at[l, 1], bh_send.at[l, 0], bh_recv.at[l, 0],
                 {"dom": prv},
             )
         ]
-        bsend[l, 1] = dot(adj_back[pl.ds(rim + rows, rim)], gagg[...]).astype(BF16)
+        bsend[l, 1] = back(1)
         halo.append(
             remote(
                 bsend.at[l, 1], brecv.at[l, 0], bh_send.at[l, 1], bh_recv.at[l, 1],
                 {"dom": nxt},
             )
         )
+        if l == 0:
+            advance(newer, 1)
         advance(older, 1)
         advance(oldest, 1)
         if l == LAYERS - 1:
             flip_agg(l)
-        if l == 0:
-            advance(newer, 1)
-        else:
+            weigh_mid(l)
+        if l > 0:
             newer = weigh(l)
         advance(oldest, 1)
 
@@ -369,6 +410,7 @@
     across = feat // 2 // 128
     piece_rows = (wide >> k) // (n // across)
     vmem = pl.BlockSpec(memory_space=pltpu.VMEM)
+    hbm = pl.BlockSpec(memory_space=pl.ANY)
     smem = pl.BlockSpec(memory_space=pltpu.SMEM)
     dma = pltpu.SemaphoreType.DMA
     scratch = [
@@ -389,6 +431,10 @@
         pltpu.VMEM((LAYERS, wide, feat), BF16),
         pltpu.VMEM((LAYERS, wide, feat), BF16),
         pltpu.VMEM((LAYERS, 2, n, piece_rows, 128), BF16),
+        pltpu.VMEM((rows, feat), BF16),
+        pltpu.VMEM(w_self.shape, BF16),
+        pltpu.VMEM(w_nbr.shape, BF16),
+        dma((3,)),
         dma((LAYERS, 2)), dma((LAYERS, 2)), dma((LAYERS, 2)), dma((LAYERS, 2)),
         dma((LAYERS, 2, k)), dma((LAYERS, 2, k)),
         dma((LAYERS, 2, n)), dma((LAYERS, 2, n)),
@@ -402,7 +448,7 @@
             jax.ShapeDtypeStruct((rows, feat), BF16),
             jax.ShapeDtypeStruct((LAYERS, wide, feat), BF16),
         ),
-        in_specs=[vmem, vmem, smem, smem, vmem, vmem, vmem],
+        in_specs=[vmem, vmem, smem, smem, hbm, hbm, hbm],
         out_specs=(vmem, vmem, vmem),
         scratch_shapes=scratch,
         compiler_params=pltpu.CompilerParams(

time: 134 us -> 132 us (0.985)
  Pallas kernels: 124 us -> 122 us
    pallas_call x1, Pallas kernels: 124 us -> 122 us  [per_device(): pl.pallas_call(functools.partial(kernel, n, k), out_shape=(jax.ShapeDtype...]
where the time goes in v3:
time: 132 us
  Pallas kernels  122 us (92%)
  other arithmetic  5.68 us (4%)
  local copies, waits for them, and re-layouts  3.3 us (2%)
    pallas_call x1, Pallas kernels, per_device(): pl.pallas_call(functools.partial(kernel, n, k), out_shape=(jax.ShapeDtype...  122 us
    mul x1, other arithmetic, per_device(): gout[:, feat:].astype(F32) * factor  5.68 us
    unnamed x7, local copies, waits for them, and re-layouts  3.3 us

profile of v3, /device:TPU:0, one launch (start us, length us, event | category | flops | bytes accessed | tf_op | source)
XLA Modules:
  0.0 132.1 jit_solution(10489962444208735759)
XLA Ops:
  0.6 1.3 %copy.11.source = s32[8,4]{1,0:T(8,128)} copy(s32[8,4]{0,1:T(4,128)} %param.9) | data formatting | bytes 256 | tf_op args[2]
  2.0 122.5 %shard_map.102 = (bf16[1024,512]{1,0:T(8,128)(2,1)}, bf16[1024,512]{1,0:T(8,128)(2,1)}, bf16[3,1024,512]{2,1,0:T(8,128)(2,1)}) custom-call(bf16[1024,512]{1,0:T(8,128)(2,1)} %bitcast.6, bf16[8,4,128,128]{3,2,1,0:T(8,128)(2,1)} %blocks.1, s32[8,4]{1,0:T(8,128)} %copy.11.source, s32[8]{0:T(128)} %count.1, bf16[1024,512]{1,0:T(8,128)(2,1)} %bitcast.7, ...), custom_call_target="tpu_custom_call" | custom-call | tf_op jit(solution)/shard_map/pallas_call | solution.py:444
  124.5 0.0 copy-start.1
  124.5 0.0 copy-start
  124.5 5.7 %convert_multiply_fusion = (f32[3,512,512]{2,1,0:T(8,128)}, f32[3,512,512]{2,1,0:T(8,128)}) fusion(bf16[3,1024,512]{2,1,0:T(8,128)(2,1)} %get-tuple-element.9), kind=kLoop, calls=%fused_computation | loop fusion | flops 3145728 | bytes 9437184 | tf_op jit(solution)/shard_map/mul | solution.py:466
  130.1 0.0 copy-done.1
  130.2 1.0 copy.14
  131.1 0.0 copy-done
  131.1 1.0 copy.15
Async XLA Ops:
  124.5 5.7 %copy-start.1 = (bf16[1024,512]{1,0:T(8,128)(2,1)S(1)}, bf16[1024,512]{1,0:T(8,128)(2,1)}, u32[]{:S(2)}) copy-start(bf16[1024,512]{1,0:T(8,128)(2,1)} %get-tuple-element.7) | copy-start | bytes 3145732
  124.5 6.7 %copy-start = (bf16[1024,512]{1,0:T(8,128)(2,1)S(1)}, bf16[1024,512]{1,0:T(8,128)(2,1)}, u32[]{:S(2)}) copy-start(bf16[1024,512]{1,0:T(8,128)(2,1)} %get-tuple-element.8) | copy-start | bytes 3145732
